TPU v7x, 32 devices: a whole 2x2x4 slice. The times are simulated.
32 devices in a mesh: freq: 4 (over z), rcv: 8 (over y, x, core).
Axes of the slice: x: 2, y: 2, z: 4, core: 2. Of those that a mesh axis runs over, the one named last changes fastest.
Arguments:
- reflection: float32 [128, 2, 1024, 2048], P('freq', None, None, 'rcv'), may hold values from -0.09375 to 0.09375
- focusing_input: float32 [128, 2, 32, 2048], P('freq', None, None, 'rcv'), may hold values from -6 to 6
- direct_wave: float32 [256, 32, 2048], P(None, 'freq', 'rcv'), may hold values from -6 to 6
- mute_source: int32 [32, 1024], P('rcv', 'freq'), may hold values from 32 to 127
- mute_receiver: int32 [32, 2048], P('freq', 'rcv'), may hold values from 32 to 127
Outputs:
- focus_minus: float32 [256, 32, 1024], P(None, 'rcv', 'freq')
- focus_plus: float32 [256, 32, 2048], P(None, 'freq', 'rcv')
All inputs are finite; a program needn't handle non-finite values.
Results may differ from a plain program's by a relative error of at most 0.00007.
Values sent between devices are 32-bit elements; how exact they have to be, the bound alone decides.
A program may use at most 192 MiB of HBM per device.

v0:
```python
import math

import jax
import jax.numpy as jnp
from jax import lax
from jax.sharding import PartitionSpec as P

MAXIMUM_ACCURACY = lax.Precision.HIGHEST


def dft_tables(freqs, samples):
    index_freq = lax.broadcasted_iota(jnp.int32, (freqs, samples), 0) + 1
    index_time = lax.broadcasted_iota(jnp.int32, (freqs, samples), 1)
    phase_turns = jnp.mod(index_freq * index_time, samples).astype(jnp.float32) * (
        2.0 * math.pi / samples
    )
    return (jnp.cos(phase_turns), jnp.sin(phase_turns))


def window(traces, mute_table):
    samples = traces.shape[0]
    time_index = lax.broadcasted_iota(jnp.int32, (samples, 1, 1), 0)
    kept_mask = (time_index < mute_table[None]) | (time_index > samples - mute_table[None])
    return jnp.where(kept_mask, traces, jnp.zeros_like(traces))


def forward_panel(reflection, focusing_input):
    reflection_real = reflection[:, 0]
    reflection_imaginary = reflection[:, 1]
    real_part = jnp.einsum(
        "ual,uel->eua", reflection_real, focusing_input[:, 0], precision=MAXIMUM_ACCURACY
    ) - jnp.einsum(
        "ual,uel->eua", reflection_imaginary, focusing_input[:, 1], precision=MAXIMUM_ACCURACY
    )
    imag_part = jnp.einsum(
        "ual,uel->eua", reflection_real, focusing_input[:, 1], precision=MAXIMUM_ACCURACY
    ) + jnp.einsum(
        "ual,uel->eua", reflection_imaginary, focusing_input[:, 0], precision=MAXIMUM_ACCURACY
    )
    return jnp.stack((real_part, imag_part), axis=2)


def adjoint_panel(reflection, receiver_panel):
    reflection_real = reflection[:, 0]
    reflection_imaginary = reflection[:, 1]
    real_part = jnp.einsum(
        "klh,lhc->klc", receiver_panel[:, :, 0], reflection_real, precision=MAXIMUM_ACCURACY
    ) + jnp.einsum(
        "klh,lhc->klc", receiver_panel[:, :, 1], reflection_imaginary, precision=MAXIMUM_ACCURACY
    )
    imag_part = jnp.einsum(
        "klh,lhc->klc", receiver_panel[:, :, 1], reflection_real, precision=MAXIMUM_ACCURACY
    ) - jnp.einsum(
        "klh,lhc->klc", receiver_panel[:, :, 0], reflection_imaginary, precision=MAXIMUM_ACCURACY
    )
    return jnp.stack((real_part, imag_part), axis=2)


def to_time(spectrum, cosine, sine_table, factor):
    return factor * (
        jnp.einsum("akb,kt->tab", spectrum[:, :, 0], cosine, precision=MAXIMUM_ACCURACY)
        - jnp.einsum("akb,kt->tab", spectrum[:, :, 1], sine_table, precision=MAXIMUM_ACCURACY)
    )


def to_freq(traces, cosine, sine_table, factor):
    real_part = factor * jnp.einsum("tab,kt->akb", traces, cosine, precision=MAXIMUM_ACCURACY)
    imag_part = -factor * jnp.einsum("tab,kt->akb", traces, sine_table, precision=MAXIMUM_ACCURACY)
    return jnp.stack((real_part, imag_part), axis=2)


def body(reflection, focusing_input, direct_wave, mute_source, mute_receiver):
    freqs = reflection.shape[0] * lax.axis_size("freq")
    samples = 2 * freqs
    factor = 1.0 / math.sqrt(freqs)
    cosine, sine_table = dft_tables(freqs, samples)
    share = mute_source.shape[0]
    term = forward_panel(reflection, focusing_input)
    summed = lax.psum(term, "rcv")
    spectrum = lax.all_to_all(summed, "freq", split_axis=3, concat_axis=1, tiled=True)
    mutes_all = lax.all_gather(mute_source, "rcv", axis=0, tiled=True)
    windowed = window(to_time(spectrum, cosine, sine_table, factor), mutes_all)
    focus_minus = lax.dynamic_slice_in_dim(windowed, lax.axis_index("rcv") * share, share, 1)
    back_local = to_freq(windowed, cosine, sine_table, factor)
    back_spec = lax.all_to_all(back_local, "freq", split_axis=1, concat_axis=3, tiled=True)
    adjoint = adjoint_panel(reflection, back_spec)
    receiver_spec = lax.all_to_all(adjoint, "freq", split_axis=0, concat_axis=1, tiled=True)
    adj_time = to_time(receiver_spec, cosine, sine_table, factor)
    focus_plus = direct_wave - window(adj_time, mute_receiver)
    return (focus_minus, focus_plus)


def solution(mesh):
    placed = (
        P("freq", None, None, "rcv"),
        P("freq", None, None, "rcv"),
        P(None, "freq", "rcv"),
        P("rcv", "freq"),
        P("freq", "rcv"),
    )
    return jax.shard_map(
        body,
        mesh=mesh,
        in_specs=placed,
        out_specs=(P(None, "rcv", "freq"), P(None, "freq", "rcv")),
        check_vma=False,
    )
```

profile of v0, /device:TPU:0, one launch (start us, length us, event | category | flops | bytes accessed | tf_op | source)
XLA Modules:
  0.0 1034.1 jit_solution(2388256514138180591)
XLA Ops:
  7.2 0.0 copy-start.2
  7.2 0.0 all-reduce.2.cloned.1.call-start
  7.2 35.6 %fusion.4 = f32[32,32,1024]{2,1,0:T(8,128)} fusion(f32[32,2,1024,256]{3,2,1,0:T(8,128)} %param.5, f32[32,2,32,256]{3,2,1,0:T(8,128)} %param.6), kind=kOutput, calls=%fused_computation.4 | convolution fusion | flops 3221225472 | bytes 38797312 | tf_op jit(solution)/shard_map/ual,uel->eua/dot_general | solution.py:37
  42.8 0.0 copy-done.2
  42.8 34.7 %fusion.6 = f32[32,32,1024]{2,1,0:T(8,128)} fusion(f32[32,2,1024,256]{3,2,1,0:T(8,128)} %param.5, f32[32,2,32,256]{3,2,1,0:T(8,128)S(1)} %copy-done.2), kind=kOutput, calls=%fused_computation.6 | convolution fusion | flops 3221225472 | bytes 38797312 | tf_op jit(solution)/shard_map/ual,uel->eua/dot_general | solution.py:32
  77.5 35.3 %add_bitcast_fusion = f32[32,32,1,1024]{3,0,1,2:T(8,128)} fusion(f32[32,32,1024]{2,1,0:T(8,128)} %fusion.4, f32[32,2,1024,256]{3,2,1,0:T(8,128)} %param.5, f32[32,2,32,256]{3,2,1,0:T(8,128)S(1)} %copy-done.2), kind=kOutput, calls=%fused_computation.39 | convolution fusion | flops 3222274048 | bytes 42991616 | tf_op jit(solution)/shard_map/ual,uel->eua/dot_general | solution.py:35
  112.8 35.0 %subtract_bitcast_fusion = f32[32,32,1,1024]{3,0,1,2:T(8,128)} fusion(f32[32,32,1024]{2,1,0:T(8,128)} %fusion.6, f32[32,2,1024,256]{3,2,1,0:T(8,128)} %param.5, f32[32,2,32,256]{3,2,1,0:T(8,128)S(1)} %copy-done.2), kind=kOutput, calls=%fused_computation.40 | convolution fusion | flops 3222274048 | bytes 42991616 | tf_op jit(solution)/shard_map/ual,uel->eua/dot_general | solution.py:30
  147.9 8.4 pad_maximum_fusion
  156.3 0.0 all-reduce.2.cloned.1.call-update
  156.3 129.4 %all-reduce.2.cloned.1.call-done = f32[32,32,2,1024]{3,0,1,2:T(8,128)} async-done(((f32[32,32,2,1024]{3,0,1,2:T(8,128)}), f32[32,32,2,1024]{3,0,1,2:T(8,128)}) %all-reduce.2.cloned.1.call-update) | async-done | bytes 8388624 | tf_op jit(solution)/shard_map/psum | solution.py:79
  285.7 26.4 %copy.23 = f32[32,32,2,1024]{0,1,2,3:T(8,128)} copy(f32[32,32,2,1024]{3,0,1,2:T(8,128)} %all-reduce.2.cloned.1.call-done) | data formatting | bytes 16777216 | tf_op jit(solution)/shard_map/psum | solution.py:79
  312.2 33.5 %reshape.16 = f32[4,1,524288]{2,1,0:T(1,128)} reshape(f32[1024,2,32,32]{3,2,1,0:T(8,128)} %bitcast.137) | data formatting | bytes 16777216
  345.6 5.8 all-to-all-start
  351.4 0.0 copy-done.5
  351.4 8.9 all-gather
  360.4 173.9 %all-to-all-done = f32[4,1,524288]{2,1,0:T(1,128)} async-done(((f32[4,1,524288]{2,1,0:T(1,128)}), f32[4,1,524288]{2,1,0:T(1,128)}, u32[]{:S(2)}, u32[]{:S(2)}) %all-to-all-start) | async-done | bytes 8388640 | tf_op jit(solution)/shard_map/all_to_all | solution.py:80
  534.3 0.5 broadcast.42
  534.8 28.4 %reduce = f32[4,524288]{1,0:T(4,128)} reduce(f32[4,1,524288]{2,1,0:T(1,128)} %all-to-all-done, f32[]{:T(128)} %broadcast.42), dimensions={1}, to_apply=%all_to_all.39.reduce_sub_computation | reduce | bytes 16777220 | tf_op jit(solution)/shard_map/all_to_all | solution.py:80
  563.2 31.1 %reshape.17 = f32[1024,2,32,32]{3,2,1,0:T(8,128)} reshape(f32[4,524288]{1,0:T(4,128)} %reduce) | data formatting | bytes 16777216
  594.3 26.6 %copy.24 = f32[32,32,2,4,256]{4,1,3,0,2:T(8,128)} copy(f32[32,32,2,4,256]{0,1,2,4,3:T(8,128)} %bitcast.138) | data formatting | bytes 16777216 | tf_op jit(solution)/shard_map/all_to_all | solution.py:80
  620.9 10.2 fusion.25
  631.1 0.0 copy-done.1
  631.1 9.4 multiply_select_fusion
  640.5 0.0 copy-start
  640.5 6.3 multiply_bitcast_fusion
  646.9 0.0 copy-done
  646.9 6.1 multiply_bitcast_fusion.1
  653.0 1.0 pad_maximum_fusion.1
  654.0 5.3 copy.27
  659.3 186.7 %all_to_all.54 = f32[32,128,2,256]{3,0,2,1:T(8,128)} all-to-all(f32[32,128,2,256]{3,0,2,1:T(8,128)S(1)} %copy.27), channel_id=1, replica_groups=mesh['freq'=4,'rcv'=8] {'freq'}, dimensions={1} | all-to-all | bytes 16777216 | tf_op jit(solution)/shard_map/all_to_all | solution.py:85
  846.0 14.6 %copy.44 = f32[32,4,32,2,256]{4,1,0,2,3:T(4,128)} copy(f32[32,4,32,2,256]{4,0,3,2,1:T(8,128)} %bitcast.141) | data formatting | bytes 16777216 | tf_op jit(solution)/shard_map/all_to_all | solution.py:85
  860.5 10.7 %all_to_all.46 = f32[32,32,2,1024]{3,0,1,2:T(8,128)} reshape(f32[32,32,2,4,256]{4,3,0,1,2:T(4,128)} %bitcast.142) | data formatting | bytes 16777216 | tf_op jit(solution)/shard_map/all_to_all | solution.py:85
  871.3 23.3 %fusion = f32[32,32,256]{2,1,0:T(8,128)S(1)} fusion(f32[32,2,1024,256]{3,2,1,0:T(8,128)} %param.5, f32[32,32,2,1024]{3,0,1,2:T(8,128)} %all_to_all.46), kind=kOutput, calls=%fused_computation | convolution fusion | flops 3221225472 | bytes 38797312 | tf_op jit(solution)/shard_map/klh,lhc->klc/dot_general | solution.py:53
  894.6 23.2 %fusion.2 = f32[32,32,256]{2,1,0:T(8,128)S(1)} fusion(f32[32,2,1024,256]{3,2,1,0:T(8,128)} %param.5, f32[32,32,2,1024]{3,0,1,2:T(8,128)} %all_to_all.46), kind=kOutput, calls=%fused_computation.2 | convolution fusion | flops 3221225472 | bytes 38797312 | tf_op jit(solution)/shard_map/klh,lhc->klc/dot_general | solution.py:48
  917.8 23.6 %fusion.41 = f32[32,32,1,256]{3,0,1,2:T(8,128)S(1)} fusion(f32[32,32,256]{2,1,0:T(8,128)S(1)} %fusion, f32[32,2,1024,256]{3,2,1,0:T(8,128)} %param.5, f32[32,32,2,1024]{3,0,1,2:T(8,128)} %all_to_all.46), kind=kOutput, calls=%fused_computation.49 | convolution fusion | flops 3221487616 | bytes 39845888 | tf_op jit(solution)/shard_map/klh,lhc->klc/dot_general | solution.py:51
  941.5 23.4 %fusion.35 = f32[32,32,1,256]{3,0,1,2:T(8,128)S(1)} fusion(f32[32,32,256]{2,1,0:T(8,128)S(1)} %fusion.2, f32[32,2,1024,256]{3,2,1,0:T(8,128)} %param.5, f32[32,32,2,1024]{3,0,1,2:T(8,128)} %all_to_all.46), kind=kOutput, calls=%fused_computation.47 | convolution fusion | flops 3221487616 | bytes 39845888 | tf_op jit(solution)/shard_map/klh,lhc->klc/dot_general | solution.py:46
  964.9 0.0 copy-start.4
  964.9 0.1 pad_maximum_fusion.2
  965.1 2.5 copy.29
  967.6 3.9 all-to-all-start.2
  971.5 0.0 copy-done.4
  971.5 1.3 constant_dynamic-slice_fusion
  972.8 1.6 copy.32
  974.4 44.2 %all-to-all-done.2 = f32[32,32,2,256]{3,1,2,0:T(8,128)S(1)} async-done(((f32[32,32,2,256]{3,1,2,0:T(8,128)}), f32[32,32,2,256]{3,1,2,0:T(8,128)S(1)}, u32[]{:S(2)}, u32[]{:S(2)}) %all-to-all-start.2) | async-done | bytes 2097184 | tf_op jit(solution)/shard_map/all_to_all | solution.py:87
  1018.7 0.1 copy.30
  1018.8 2.3 fusion.44
  1021.1 3.2 copy_subtract_fusion
  1024.3 2.5 copy.33
  (8 shorter events, 0.0 us)
Async XLA Ops:
  7.2 35.7 %copy-start.2 = (f32[32,2,32,256]{3,2,1,0:T(8,128)S(1)}, f32[32,2,32,256]{3,2,1,0:T(8,128)}, u32[]{:S(2)}) copy-start(f32[32,2,32,256]{3,2,1,0:T(8,128)} %param.6) | copy-start | bytes 6291460
  7.2 278.6 %all-reduce.2.cloned.1.call-start = ((), (), s32[]{:S(2)}) async-start(), calls=%async_computation.3 | async-start | bytes 16777216 | tf_op jit(solution)/shard_map/psum | solution.py:79
  345.6 5.8 copy-start.5
  345.6 188.7 %all-to-all-start = ((f32[4,1,524288]{2,1,0:T(1,128)}), f32[4,1,524288]{2,1,0:T(1,128)}, u32[]{:S(2)}, u32[]{:S(2)}) async-start(f32[4,1,524288]{2,1,0:T(1,128)} %reshape.16), calls=%async_computation | async-start | bytes 16777216 | tf_op jit(solution)/shard_map/all_to_all | solution.py:80
  620.9 10.2 copy-start.1
  640.5 6.4 copy-start
  964.9 6.6 copy-start.4
  967.6 51.1 %all-to-all-start.2 = ((f32[32,32,2,256]{3,1,2,0:T(8,128)}), f32[32,32,2,256]{3,1,2,0:T(8,128)S(1)}, u32[]{:S(2)}, u32[]{:S(2)}) async-start(f32[32,32,2,256]{3,1,2,0:T(8,128)} %copy.29), calls=%async_computation.2 | async-start | bytes 4194304 | tf_op jit(solution)/shard_map/all_to_all | solution.py:87
  1018.7 2.4 copy-start.3
Sparse Core Ops, SparseCore 0:
  156.4 129.2 all-reduce.1
where the time goes:
time: 1040 us; the launch traced here: 1030 us
  waiting for transfers between devices  348 us (33%)
  matrix products  272 us (26%)
  blocking collectives  196 us (19%)
  local copies, waits for them, and re-layouts  157 us (15%)
  other arithmetic  37.9 us (4%)
  between operations  14.7 us (1%)
    all_to_all x1, blocking collectives, body(): lax.all_to_all(back_local, 'freq', split_axis=1, concat_axis=3, tiled=True)  187 us
    all_to_all x1, waiting for transfers between devices, body(): lax.all_to_all(summed, 'freq', split_axis=3, concat_axis=1, tiled=True)  174 us
    psum x1, waiting for transfers between devices, body(): summed = lax.psum(term, 'rcv')  129 us
    unnamed x17, local copies, waits for them, and re-layouts  68.8 us
    all_to_all x1, waiting for transfers between devices, body(): lax.all_to_all(adjoint, 'freq', split_axis=0, concat_axis=1, tiled=True)  44.2 us
    dot_general x1, matrix products, forward_panel(): jnp.einsum('ual,uel->eua', reflection_imaginary, focusing_input[:, 0], pr...  35.6 us
    dot_general x1, matrix products, forward_panel(): jnp.einsum('ual,uel->eua', reflection_real, focusing_input[:, 1], precisi...  35.3 us
    dot_general x1, matrix products, forward_panel(): jnp.einsum('ual,uel->eua', reflection_real, focusing_input[:, 0], precisi...  35 us
  transfers between devices with their start and end apart: 3, of which 3 were waited for; matrix products, arithmetic and copies ran while one was open for 0% of the time, Pallas kernels for 0%

commit v1 on v0

v1 whole, which is shorter than its diff:
```python
import functools
import math

import jax
import jax.numpy as jnp
import ml_dtypes
import numpy as np
from jax import lax
from jax.experimental import pallas as pl
from jax.experimental.pallas import tpu as pltpu
from jax.sharding import PartitionSpec as P

LIMIT = 40 * 1024 * 1024
LANES = 128


def split(value):
    high = value.astype(jnp.bfloat16)
    low = (value - high.astype(jnp.float32)).astype(jnp.bfloat16)
    return high, low


def dot(a, b):
    return jnp.dot(a, b, preferred_element_type=jnp.float32)


def dot_nt(a, b):
    return lax.dot_general(a, b, (((1,), (1,)), ((), ())), preferred_element_type=jnp.float32)


def left3(stacked, high, matrix, product):
    rows = high.shape[0]
    matrix_high, matrix_low = split(matrix)
    both = product(stacked, matrix_high)
    return both[:rows] + both[rows:] + product(high, matrix_low)


def table3(table_high, table_low, value):
    value_high, value_low = split(value)
    return dot(table_high, value_high) + dot(table_low, value_high) + dot(table_high, value_low)


def turned(value, share, sign):
    rows = value.shape[0]
    row = lax.broadcasted_iota(jnp.int32, value.shape, 0)
    is_real = row % (2 * share) < share
    from_imag = pltpu.roll(value, rows - share, 0)
    from_real = pltpu.roll(value, share, 0)
    return jnp.where(is_real, -sign * from_imag, sign * from_real)


def forward_kernel(share, refl_ref, focus_ref, out_ref):
    groups, parts, steps, rows, width = out_ref.shape
    for step in range(steps):
        high, low = split(focus_ref[step])
        stacked = jnp.concatenate([high, low], axis=0)
        real, imag = (
            left3(stacked, high, refl_ref[step, c].reshape(parts * width, -1), dot_nt)
            for c in (0, 1)
        )
        panel = real + turned(imag, share, 1.0)
        for part in range(parts):
            out_ref[:, part, step] = panel[:, part * width : (part + 1) * width].reshape(
                groups, rows, width
            )


def forward(refl, focus, chunk, width, groups, share):
    freqs, _, parts, _, receivers = refl.shape
    steps = 2
    return pl.pallas_call(
        functools.partial(forward_kernel, share),
        grid=(freqs // steps,),
        in_specs=[
            pl.BlockSpec((steps, 2, parts, width, receivers), lambda k: (k, 0, 0, chunk, 0)),
            pl.BlockSpec((steps, groups * 2 * share, receivers), lambda k: (k, 0, 0)),
        ],
        out_specs=pl.BlockSpec(
            (groups, parts, steps, 2 * share, width), lambda k: (0, 0, k, 0, 0)
        ),
        out_shape=jax.ShapeDtypeStruct(
            (groups, parts, freqs, 2 * share, width), jnp.float32
        ),
        compiler_params=pltpu.CompilerParams(vmem_limit_bytes=LIMIT),
        cost_estimate=pl.CostEstimate(
            flops=6 * 2 * freqs * 2 * parts * width * receivers * groups * 2 * share,
            bytes_accessed=4 * freqs * 2 * parts * width * (receivers + groups * share),
            transcendentals=0,
        ),
        name="forward",
    )(refl, focus)


def adjoint_kernel(share, refl_ref, spec_ref, *rest):
    prev_ref, out_ref = rest if len(rest) == 2 else (None, rest[0])
    groups, parts, steps, rows, width = spec_ref.shape
    for step in range(steps):
        spec = jnp.concatenate(
            [spec_ref[:, part, step].reshape(groups * rows, width) for part in range(parts)],
            axis=1,
        )
        high, low = split(spec)
        stacked = jnp.concatenate([high, low], axis=0)
        real, imag = (
            left3(stacked, high, refl_ref[step, c].reshape(parts * width, -1), dot)
            for c in (0, 1)
        )
        panel = (real + turned(imag, share, -1.0)).reshape(out_ref[:, step].shape)
        if prev_ref is not None:
            panel = panel + prev_ref[:, step]
        out_ref[:, step] = panel


def adjoint(refl, spec, prev, chunk, width, groups, share):
    freqs, _, parts, _, receivers = refl.shape
    steps = 2
    shape = (parts, freqs, groups // parts, 2 * share, receivers)
    out_spec = pl.BlockSpec(
        (parts, steps, groups // parts, 2 * share, receivers), lambda k: (0, k, 0, 0, 0)
    )
    more = [] if prev is None else [prev]
    return pl.pallas_call(
        functools.partial(adjoint_kernel, share),
        grid=(freqs // steps,),
        in_specs=[
            pl.BlockSpec((steps, 2, parts, width, receivers), lambda k: (k, 0, 0, chunk, 0)),
            pl.BlockSpec(
                (groups, parts, steps, 2 * share, width), lambda k: (0, 0, k, 0, 0)
            ),
        ]
        + [out_spec] * len(more),
        out_specs=out_spec,
        out_shape=jax.ShapeDtypeStruct(shape, jnp.float32),
        compiler_params=pltpu.CompilerParams(vmem_limit_bytes=LIMIT),
        cost_estimate=pl.CostEstimate(
            flops=6 * 2 * freqs * 2 * parts * width * receivers * groups * 2 * share,
            bytes_accessed=4 * freqs * 2 * parts * width * (receivers + groups * share),
            transcendentals=0,
        ),
        name="adjoint",
    )(refl, spec, *more)


def kept(samples, mute, width):
    time = lax.broadcasted_iota(jnp.int32, (samples, width), 0)
    return (time < mute) | (time > samples - mute)


def window_kernel(share, to_time, to_freq, mute_ref, spec_ref, *rest):
    trace_ref, back_ref = rest[-2:]
    freqs, _, width = spec_ref.shape
    samples = 2 * freqs
    for point in range(share):
        spec = jnp.concatenate([spec_ref[:, point, :], spec_ref[:, share + point, :]], axis=0)
        trace = table3(to_time[0], to_time[1], spec)
        trace = jnp.where(kept(samples, mute_ref[point : point + 1, :], width), trace, 0.0)
        trace_ref[:, point, :] = trace
        back = table3(to_freq[0], to_freq[1], trace)
        back_ref[:, point, :] = back[:freqs]
        back_ref[:, share + point, :] = back[freqs:]


def window_source(to_time, to_freq, mute, spec, traces, chunk, width, share):
    freqs = spec.shape[0]
    samples = 2 * freqs
    more = [] if traces is None else [traces]
    whole = lambda k: (0, 0, 0)
    return pl.pallas_call(
        functools.partial(window_kernel, share),
        grid=(1,),
        in_specs=[
            pl.BlockSpec(to_time.shape, whole),
            pl.BlockSpec(to_freq.shape, whole),
            pl.BlockSpec((share, width), lambda k: (0, chunk)),
            pl.BlockSpec(spec.shape, whole),
        ]
        + [pl.BlockSpec(memory_space=pl.ANY)] * len(more),
        out_specs=[
            pl.BlockSpec((samples, share, width), lambda k: (0, 0, chunk)),
            pl.BlockSpec(spec.shape, whole),
        ],
        out_shape=[
            jax.ShapeDtypeStruct((samples, share, mute.shape[1]), jnp.float32),
            jax.ShapeDtypeStruct(spec.shape, jnp.float32),
        ],
        input_output_aliases={4: 0} if more else {},
        compiler_params=pltpu.CompilerParams(vmem_limit_bytes=LIMIT),
        cost_estimate=pl.CostEstimate(
            flops=3 * 4 * samples * samples * share * width,
            bytes_accessed=4 * 3 * samples * share * width,
            transcendentals=0,
        ),
        name="window_source",
    )(to_time, to_freq, mute, spec, *more)


def final_kernel(share, to_time, mute_ref, spec_ref, direct_ref, out_ref):
    freqs, _, width = spec_ref.shape
    samples = 2 * freqs
    for point in range(out_ref.shape[1]):
        row = point // share * 2 * share + point % share
        spec = jnp.concatenate([spec_ref[:, row, :], spec_ref[:, row + share, :]], axis=0)
        trace = table3(to_time[0], to_time[1], spec)
        trace = jnp.where(kept(samples, mute_ref[point : point + 1, :], width), trace, 0.0)
        out_ref[:, point, :] = direct_ref[:, point, :] - trace


def final(to_time, mute, spec, direct, share):
    samples, points, receivers = direct.shape
    freqs, rows, _ = spec.shape
    width = min(LANES, receivers)
    return pl.pallas_call(
        functools.partial(final_kernel, share),
        grid=(receivers // width,),
        in_specs=[
            pl.BlockSpec(to_time.shape, lambda k: (0, 0, 0)),
            pl.BlockSpec((points, width), lambda k: (0, k)),
            pl.BlockSpec((freqs, rows, width), lambda k: (0, 0, k)),
            pl.BlockSpec((samples, points, width), lambda k: (0, 0, k)),
        ],
        out_specs=pl.BlockSpec((samples, points, width), lambda k: (0, 0, k)),
        out_shape=jax.ShapeDtypeStruct(direct.shape, jnp.float32),
        compiler_params=pltpu.CompilerParams(vmem_limit_bytes=LIMIT),
        cost_estimate=pl.CostEstimate(
            flops=3 * 2 * samples * samples * points * receivers,
            bytes_accessed=4 * 3 * samples * points * receivers,
            transcendentals=0,
        ),
        name="final",
    )(to_time, mute, spec, direct)


def tables(freqs):
    samples = 2 * freqs
    turns = (np.arange(1, freqs + 1)[:, None] * np.arange(samples)[None, :]) % samples
    phase = turns * (2.0 * np.pi / samples)
    whole = np.concatenate([np.cos(phase), -np.sin(phase)], axis=0) / math.sqrt(freqs)
    high = whole.astype(ml_dtypes.bfloat16)
    low = (whole - high.astype(np.float64)).astype(ml_dtypes.bfloat16)
    both = np.stack([high, low])
    return jnp.asarray(np.ascontiguousarray(both.transpose(0, 2, 1))), jnp.asarray(both)


def body(reflection, focusing_input, direct_wave, mute_source, mute_receiver):
    freq_devices = lax.axis_size("freq")
    groups = lax.axis_size("rcv")
    local, _, sources, receivers = reflection.shape
    freqs = local * freq_devices
    share, own = mute_source.shape
    points = share * groups
    width = min(LANES, own)
    chunks = own // width
    to_time, to_freq = tables(freqs)
    refl = reflection.reshape(local, 2, freq_devices, own, receivers)
    focus = focusing_input.reshape(local, 2, groups, share, receivers)
    focus = focus.transpose(0, 2, 1, 3, 4).reshape(local, 2 * points, receivers)

    specs = []
    for chunk in range(chunks):
        term = forward(refl, focus, chunk, width, groups, share)
        summed = lax.psum_scatter(term, "rcv", scatter_dimension=0, tiled=False)
        spec = lax.all_to_all(summed, "freq", split_axis=0, concat_axis=0, tiled=True)
        specs.append(spec.reshape(freqs, 2 * share, width))
    traces = None
    gathered = []
    for chunk in range(chunks):
        traces, back = window_source(
            to_time, to_freq, mute_source, specs[chunk], traces, chunk, width, share
        )
        back = back.reshape(freq_devices, local, 2 * share, width)
        back = lax.all_to_all(back, "freq", split_axis=0, concat_axis=0, tiled=True)
        gathered.append(lax.all_gather(back, "rcv", axis=0, tiled=False))
    panel = None
    for chunk in range(chunks):
        panel = adjoint(refl, gathered[chunk], panel, chunk, width, groups, share)
    panel = lax.all_to_all(panel, "freq", split_axis=0, concat_axis=0, tiled=True)
    panel = panel.reshape(freqs, groups // freq_devices * 2 * share, receivers)
    return traces, final(to_time, mute_receiver, panel, direct_wave, share)


def solution(mesh):
    placed = (
        P("freq", None, None, "rcv"),
        P("freq", None, None, "rcv"),
        P(None, "freq", "rcv"),
        P("rcv", "freq"),
        P("freq", "rcv"),
    )
    return jax.shard_map(
        body,
        mesh=mesh,
        in_specs=placed,
        out_specs=(P(None, "rcv", "freq"), P(None, "freq", "rcv")),
        check_vma=False,
    )
```

time: 1040 us -> 311 us (0.30)
  waiting for transfers between devices: 348 us -> 64.2 us
  matrix products: 272 us -> 0 us
  local copies, waits for them, and re-layouts: 157 us -> 13.9 us
  Pallas kernels: 0 us -> 92.3 us
  blocking collectives: 196 us -> 125 us
  other arithmetic: 37.9 us -> 0 us
    dot_general x14 -> x0, matrix products: 272 us -> none  [the longest x1 35.6 us: forward_panel(): jnp.einsum('ual,uel->eua', reflection_imaginary, focusing_input[:, 0], pr...]
    all_to_all x2 -> x0, waiting for transfers between devices: 218 us -> none  [the longest x1 174 us: body(): lax.all_to_all(summed, 'freq', split_axis=3, concat_axis=1, tiled=True)]
    psum x1 -> x0, waiting for transfers between devices: 129 us -> none  [body(): summed = lax.psum(term, 'rcv')]
    pallas_call x0 -> x7, Pallas kernels: none -> 92.3 us  [the longest x2 43 us: forward(): pl.pallas_call(functools.partial(forward_kernel, share), grid=(freqs // s...]
    all_to_all x1 -> x5, blocking collectives: 187 us -> 125 us  [the longest x1 53.1 us: body(): lax.all_to_all(panel, 'freq', split_axis=0, concat_axis=0, tiled=True)]
    unnamed x17 -> x18, local copies, waits for them, and re-layouts: 68.8 us -> 8.32 us
    all_to_all x5 -> x0, local copies, waits for them, and re-layouts: 52.5 us -> none  [the longest x2 27.1 us: body(): lax.all_to_all(summed, 'freq', split_axis=3, concat_axis=1, tiled=True)]
    reduce_scatter x0 -> x2, waiting for transfers between devices: none -> 46.8 us  [body(): summed = lax.psum_scatter(term, 'rcv', scatter_dimension=0, tiled=False)]
  transfers between devices with their start and end apart: 3 -> 4, of which waited for: 3 -> 4; matrix products, arithmetic and copies ran while one was open for 0% -> 0% of each run, Pallas kernels for 0% -> 15%
where the time goes in v1:
time: 311 us; the launch traced here: 309 us
  blocking collectives  125 us (40%)
  Pallas kernels  92.3 us (30%)
  waiting for transfers between devices  64.2 us (21%)
  local copies, waits for them, and re-layouts  13.9 us (4%)
  between operations  13.9 us (4%)
    all_to_all x1, blocking collectives, body(): lax.all_to_all(panel, 'freq', split_axis=0, concat_axis=0, tiled=True)  53.1 us
    reduce_scatter x2, waiting for transfers between devices, body(): summed = lax.psum_scatter(term, 'rcv', scatter_dimension=0, tiled=False)  46.8 us
    pallas_call x2, Pallas kernels, forward(): pl.pallas_call(functools.partial(forward_kernel, share), grid=(freqs // s...  43 us
    all_to_all x2, blocking collectives, body(): lax.all_to_all(summed, 'freq', split_axis=0, concat_axis=0, tiled=True)  38.2 us
    pallas_call x2, Pallas kernels, adjoint(): pl.pallas_call(functools.partial(adjoint_kernel, share), grid=(freqs // s...  38.1 us
    all_to_all x2, blocking collectives, body(): back = lax.all_to_all(back, 'freq', split_axis=0, concat_axis=0, tiled=True)  33.5 us
    all_gather x2, waiting for transfers between devices, body(): gathered.append(lax.all_gather(back, 'rcv', axis=0, tiled=False))  17.3 us
    unnamed x18, local copies, waits for them, and re-layouts  8.32 us
  transfers between devices with their start and end apart: 4, of which 4 were waited for; matrix products, arithmetic and copies ran while one was open for 0% of the time, Pallas kernels for 15%

profile of v1, /device:TPU:0, one launch (start us, length us, event | category | flops | bytes accessed | tf_op | source)
XLA Modules:
  0.0 309.3 jit_solution(10211933461511564329)
XLA Ops:
  7.2 0.0 reduce-scatter.5.cloned.1.call-start
  7.2 1.9 reshape.29
  9.1 1.8 copy.13
  10.8 2.0 reshape.30.focus_ref
  12.8 21.2 %forward.3 = f32[8,4,32,8,128]{4,3,2,1,0:T(8,128)S(1)} custom-call(f32[32,2,4,256,256]{4,3,2,1,0:T(8,128)} %bitcast.refl_ref, f32[32,64,256]{2,1,0:T(8,128)S(1)} %reshape.30.focus_ref), custom_call_target="tpu_custom_call" | custom-call | flops 6442450944 | bytes 37748736 | tf_op jit(solution)/shard_map/forward/pallas_call | solution.py:71
  34.0 0.0 copy-start.1
  34.1 2.0 copy-done.1
  36.0 0.0 reduce-scatter.5.cloned.1.call-update
  36.0 0.0 reduce-scatter.3.cloned.1.call-start
  36.1 21.8 %forward.2 = f32[8,4,32,8,128]{4,3,2,1,0:T(8,128)S(1)} custom-call(f32[32,2,4,256,256]{4,3,2,1,0:T(8,128)} %bitcast.refl_ref, f32[32,64,256]{2,1,0:T(8,128)S(1)} %reshape.30.focus_ref), custom_call_target="tpu_custom_call" | custom-call | flops 6442450944 | bytes 37748736 | tf_op jit(solution)/shard_map/forward/pallas_call | solution.py:71
  57.9 0.0 copy-start
  57.9 2.0 copy-done
  59.9 0.0 copy-start.5
  59.9 0.0 copy-start.6
  59.9 0.0 copy-start.8
  59.9 0.0 reduce-scatter.3.cloned.1.call-update
  59.9 0.0 all-gather.7.cloned.1.call-start
  60.0 30.2 %reduce-scatter.5.cloned.1.call-done = f32[1,4,32,8,128]{4,3,2,1,0:T(8,128)} async-done(((f32[8,4,32,8,128]{4,3,2,1,0:T(8,128)}), f32[1,4,32,8,128]{4,3,2,1,0:T(8,128)}) %reduce-scatter.5.cloned.1.call-update) | async-done | bytes 524304 | tf_op jit(solution)/shard_map/reduce_scatter | solution.py:261
  90.2 19.1 %all_to_all.25 = f32[4,32,8,128]{3,2,1,0:T(8,128)S(1)} all-to-all(f32[4,32,8,128]{3,2,1,0:T(8,128)} %bitcast.24), channel_id=1, replica_groups=mesh['freq'=4,'rcv'=8] {'freq'}, dimensions={0} | all-to-all | bytes 1048576 | tf_op jit(solution)/shard_map/all_to_all | solution.py:262
  109.3 0.0 copy-done.5
  109.3 0.0 copy-done.6
  109.3 0.0 copy-done.8
  109.3 2.6 window_source.2
  111.9 16.7 %all_to_all.26 = f32[4,32,8,128]{3,2,1,0:T(8,128)} all-to-all(f32[4,32,8,128]{3,2,1,0:T(8,128)S(1)} %bitcast.21), channel_id=1, replica_groups=mesh['freq'=4,'rcv'=8] {'freq'}, dimensions={0} | all-to-all | bytes 1048576 | tf_op jit(solution)/shard_map/all_to_all | solution.py:271
  128.6 0.0 all-gather.7.cloned.1.call-update
  128.6 0.0 all-gather.5.cloned.1.call-start
  128.7 16.6 %reduce-scatter.3.cloned.1.call-done = f32[1,4,32,8,128]{4,3,2,1,0:T(8,128)} async-done(((f32[8,4,32,8,128]{4,3,2,1,0:T(8,128)}), f32[1,4,32,8,128]{4,3,2,1,0:T(8,128)}) %reduce-scatter.3.cloned.1.call-update) | async-done | bytes 524304 | tf_op jit(solution)/shard_map/reduce_scatter | solution.py:261
  145.3 19.1 %all_to_all.27 = f32[4,32,8,128]{3,2,1,0:T(8,128)S(1)} all-to-all(f32[4,32,8,128]{3,2,1,0:T(8,128)} %bitcast.23), channel_id=1, replica_groups=mesh['freq'=4,'rcv'=8] {'freq'}, dimensions={0} | all-to-all | bytes 1048576 | tf_op jit(solution)/shard_map/all_to_all | solution.py:262
  164.4 2.6 window_source.3
  166.9 16.8 %all_to_all.28 = f32[4,32,8,128]{3,2,1,0:T(8,128)} all-to-all(f32[4,32,8,128]{3,2,1,0:T(8,128)S(1)} %bitcast.19), channel_id=1, replica_groups=mesh['freq'=4,'rcv'=8] {'freq'}, dimensions={0} | all-to-all | bytes 1048576 | tf_op jit(solution)/shard_map/all_to_all | solution.py:271
  183.7 0.0 all-gather.5.cloned.1.call-update
  183.7 0.2 all-gather.7.cloned.1.call-done
  183.9 0.0 copy-start.2
  183.9 2.2 copy-done.2
  186.1 19.2 %adjoint.2.rest_0_ = f32[4,32,2,8,256]{4,3,2,1,0:T(8,128)S(1)} custom-call(f32[32,2,4,256,256]{4,3,2,1,0:T(8,128)} %bitcast.refl_ref, f32[8,4,32,8,128]{4,3,2,1,0:T(8,128)S(1)} %bitcast.16), custom_call_target="tpu_custom_call" | custom-call | flops 6442450944 | bytes 37748736 | tf_op jit(solution)/shard_map/adjoint/pallas_call | solution.py:122
  205.3 17.1 %all-gather.5.cloned.1.call-done = f32[32,32,8,128]{3,2,1,0:T(8,128)} async-done(((f32[4,32,8,128]{3,2,1,0:T(8,128)}), f32[32,32,8,128]{3,2,1,0:T(8,128)}) %all-gather.5.cloned.1.call-update) | async-done | bytes 4194320 | tf_op jit(solution)/shard_map/all_gather | solution.py:272
  222.4 0.0 copy-start.3
  222.4 2.2 copy-done.3
  224.6 18.9 %adjoint.3 = f32[4,32,2,8,256]{4,3,2,1,0:T(8,128)S(1)} custom-call(f32[32,2,4,256,256]{4,3,2,1,0:T(8,128)} %bitcast.refl_ref, f32[8,4,32,8,128]{4,3,2,1,0:T(8,128)S(1)} %bitcast.17, f32[4,32,2,8,256]{4,3,2,1,0:T(8,128)S(1)} %adjoint.2.rest_0_), custom_call_target="tpu_custom_call" | custom-call | flops 6442450944 | bytes 37748736 | tf_op jit(solution)/shard_map/adjoint/pallas_call | solution.py:122
  243.6 0.0 copy-start.4
  243.6 0.0 copy-start.7
  243.6 53.1 %all_to_all.29 = f32[4,32,2,8,256]{4,3,2,1,0:T(8,128)S(1)} all-to-all(f32[4,32,2,8,256]{4,3,2,1,0:T(8,128)S(1)} %adjoint.3), channel_id=1, replica_groups=mesh['freq'=4,'rcv'=8] {'freq'}, dimensions={0} | all-to-all | bytes 4194304 | tf_op jit(solution)/shard_map/all_to_all | solution.py:276
  296.7 0.0 copy-done.4
  296.7 0.0 copy-done.7
  296.7 6.0 %final.1 = f32[256,8,256]{2,1,0:T(8,128)} custom-call(bf16[2,256,256]{2,1,0:T(8,128)(2,1)S(1)} %copy-done.5, s32[8,256]{1,0:T(8,128)S(1)} %copy-done.7, f32[128,16,256]{2,1,0:T(8,128)S(1)} %bitcast.15, f32[256,8,256]{2,1,0:T(8,128)S(1)} %copy-done.4), custom_call_target="tpu_custom_call" | custom-call | flops 805306368 | bytes 6291456 | tf_op jit(solution)/shard_map/final/pallas_call | solution.py:212
Async XLA Ops:
  7.2 83.0 %reduce-scatter.5.cloned.1.call-start = ((), (), s32[]{:S(2)}) async-start(), calls=%async_computation.8 | async-start | bytes 4718592 | tf_op jit(solution)/shard_map/reduce_scatter | solution.py:261
  34.0 2.0 copy-start.1
  36.0 109.2 %reduce-scatter.3.cloned.1.call-start = ((), (), s32[]{:S(2)}) async-start(), calls=%async_computation.7 | async-start | bytes 4718592 | tf_op jit(solution)/shard_map/reduce_scatter | solution.py:261
  57.9 2.0 copy-start
  59.9 49.4 %copy-start.5 = (bf16[2,256,256]{2,1,0:T(8,128)(2,1)S(1)}, bf16[2,256,256]{2,1,0:T(8,128)(2,1)}, u32[]{:S(2)}) copy-start(bf16[2,256,256]{2,1,0:T(8,128)(2,1)} %constant.4.clone.to_time) | copy-start | bytes 786436
  59.9 49.4 %copy-start.6 = (bf16[2,256,256]{2,1,0:T(8,128)(2,1)S(1)}, bf16[2,256,256]{2,1,0:T(8,128)(2,1)}, u32[]{:S(2)}) copy-start(bf16[2,256,256]{2,1,0:T(8,128)(2,1)} %constant.5.clone.to_freq) | copy-start | bytes 786436
  59.9 49.4 %copy-start.8 = (s32[4,256]{1,0:T(4,128)S(1)}, s32[4,256]{1,0:T(4,128)}, u32[]{:S(2)}) copy-start(s32[4,256]{1,0:T(4,128)} %mute_ref.4) | copy-start | bytes 12292
  59.9 124.0 %all-gather.7.cloned.1.call-start = ((), (), s32[]{:S(2)}) async-start(), calls=%async_computation.10 | async-start | bytes 4718592 | tf_op jit(solution)/shard_map/all_gather | solution.py:272
  128.6 93.8 %all-gather.5.cloned.1.call-start = ((), (), s32[]{:S(2)}) async-start(), calls=%async_computation.9 | async-start | bytes 4718592 | tf_op jit(solution)/shard_map/all_gather | solution.py:272
  183.9 2.2 copy-start.2
  222.4 2.2 copy-start.3
  243.6 53.2 %copy-start.4 = (f32[256,8,256]{2,1,0:T(8,128)S(1)}, f32[256,8,256]{2,1,0:T(8,128)}, u32[]{:S(2)}) copy-start(f32[256,8,256]{2,1,0:T(8,128)} %direct_ref.1) | copy-start | bytes 6291460
  243.6 53.2 %copy-start.7 = (s32[8,256]{1,0:T(8,128)S(1)}, s32[8,256]{1,0:T(8,128)}, u32[]{:S(2)}) copy-start(s32[8,256]{1,0:T(8,128)} %mute_ref.5) | copy-start | bytes 24580
Sparse Core Ops, SparseCore 0:
  36.2 53.9 reduce-scatter.4
  93.9 51.3 reduce-scatter.2
  147.2 36.6 all-gather.6
  185.7 36.7 all-gather.4

commit v2 on v1

--- a/solution.py
+++ b/solution.py
@@ -49,10 +49,13 @@
     return jnp.where(is_real, -sign * from_imag, sign * from_real)
 
 
-def forward_kernel(share, refl_ref, focus_ref, out_ref):
-    groups, parts, steps, rows, width = out_ref.shape
+def forward_kernel(share, me_ref, refl_ref, focus_ref, keep_ref, send_ref):
+    half, parts, steps, rows, width = keep_ref.shape
+    groups = 2 * half
+    order = [*range(0, groups, 2), *range(1, groups, 2)]
     for step in range(steps):
-        high, low = split(focus_ref[step])
+        focus = jnp.concatenate([focus_ref[step, g ^ me_ref[0]] for g in order], axis=0)
+        high, low = split(focus)
         stacked = jnp.concatenate([high, low], axis=0)
         real, imag = (
             left3(stacked, high, refl_ref[step, c].reshape(parts * width, -1), dot_nt)
@@ -60,27 +63,30 @@
         )
         panel = real + turned(imag, share, 1.0)
         for part in range(parts):
-            out_ref[:, part, step] = panel[:, part * width : (part + 1) * width].reshape(
-                groups, rows, width
-            )
-
-
-def forward(refl, focus, chunk, width, groups, share):
+            block = panel[:, part * width : (part + 1) * width].reshape(groups, rows, width)
+            keep_ref[:, part, step] = block[:half]
+            send_ref[:, part, step] = block[half:]
+
+
+def forward(me, refl, focus, chunk, width, groups, share):
     freqs, _, parts, _, receivers = refl.shape
     steps = 2
     return pl.pallas_call(
         functools.partial(forward_kernel, share),
         grid=(freqs // steps,),
         in_specs=[
+            pl.BlockSpec(memory_space=pltpu.SMEM),
             pl.BlockSpec((steps, 2, parts, width, receivers), lambda k: (k, 0, 0, chunk, 0)),
-            pl.BlockSpec((steps, groups * 2 * share, receivers), lambda k: (k, 0, 0)),
+            pl.BlockSpec((steps, groups, 2 * share, receivers), lambda k: (k, 0, 0, 0)),
         ],
-        out_specs=pl.BlockSpec(
-            (groups, parts, steps, 2 * share, width), lambda k: (0, 0, k, 0, 0)
-        ),
-        out_shape=jax.ShapeDtypeStruct(
-            (groups, parts, freqs, 2 * share, width), jnp.float32
-        ),
+        out_specs=[
+            pl.BlockSpec((groups // 2, parts, steps, 2 * share, width), lambda k: (0, 0, k, 0, 0))
+        ]
+        * 2,
+        out_shape=[
+            jax.ShapeDtypeStruct((groups // 2, parts, freqs, 2 * share, width), jnp.float32)
+        ]
+        * 2,
         compiler_params=pltpu.CompilerParams(vmem_limit_bytes=LIMIT),
         cost_estimate=pl.CostEstimate(
             flops=6 * 2 * freqs * 2 * parts * width * receivers * groups * 2 * share,
@@ -88,17 +94,24 @@
             transcendentals=0,
         ),
         name="forward",
-    )(refl, focus)
-
-
-def adjoint_kernel(share, refl_ref, spec_ref, *rest):
+    )(me, refl, focus)
+
+
+def adjoint_kernel(share, me_ref, refl_ref, own_ref, other_ref, *rest):
     prev_ref, out_ref = rest if len(rest) == 2 else (None, rest[0])
-    groups, parts, steps, rows, width = spec_ref.shape
+    half, parts, steps, rows, width = own_ref.shape
+    odd = me_ref[0] % 2 == 1
+    pair = me_ref[0] // 2
     for step in range(steps):
-        spec = jnp.concatenate(
-            [spec_ref[:, part, step].reshape(groups * rows, width) for part in range(parts)],
-            axis=1,
-        )
+        columns = []
+        for part in range(parts):
+            pieces = []
+            for g in range(half):
+                own = own_ref[g ^ pair, part, step]
+                other = other_ref[g ^ pair, part, step]
+                pieces += [jnp.where(odd, other, own), jnp.where(odd, own, other)]
+            columns.append(jnp.concatenate(pieces, axis=0))
+        spec = jnp.concatenate(columns, axis=1)
         high, low = split(spec)
         stacked = jnp.concatenate([high, low], axis=0)
         real, imag = (
@@ -111,7 +124,7 @@
         out_ref[:, step] = panel
 
 
-def adjoint(refl, spec, prev, chunk, width, groups, share):
+def adjoint(me, refl, own, other, prev, chunk, width, groups, share):
     freqs, _, parts, _, receivers = refl.shape
     steps = 2
     shape = (parts, freqs, groups // parts, 2 * share, receivers)
@@ -123,11 +136,13 @@
         functools.partial(adjoint_kernel, share),
         grid=(freqs // steps,),
         in_specs=[
+            pl.BlockSpec(memory_space=pltpu.SMEM),
             pl.BlockSpec((steps, 2, parts, width, receivers), lambda k: (k, 0, 0, chunk, 0)),
-            pl.BlockSpec(
-                (groups, parts, steps, 2 * share, width), lambda k: (0, 0, k, 0, 0)
-            ),
-        ]
+        ]
+        + [
+            pl.BlockSpec((groups // 2, parts, steps, 2 * share, width), lambda k: (0, 0, k, 0, 0))
+        ]
+        * 2
         + [out_spec] * len(more),
         out_specs=out_spec,
         out_shape=jax.ShapeDtypeStruct(shape, jnp.float32),
@@ -138,7 +153,7 @@
             transcendentals=0,
         ),
         name="adjoint",
-    )(refl, spec, *more)
+    )(me, refl, own, other, *more)
 
 
 def kept(samples, mute, width):
@@ -241,24 +256,68 @@
     return jnp.asarray(np.ascontiguousarray(both.transpose(0, 2, 1))), jnp.asarray(both)
 
 
+def swap(value, groups, bit):
+    return lax.ppermute(value, "rcv", [(i, i ^ (1 << bit)) for i in range(groups)])
+
+
+def scatter_half(value, groups, bits):
+    rest = list(bits)
+    while rest:
+        bit = rest.pop(0)
+        axis = sum(b > bit for b in rest)
+        mine = lax.index_in_dim(value, 0, axis, keepdims=False)
+        value = mine + swap(lax.index_in_dim(value, 1, axis, keepdims=False), groups, bit)
+    return value
+
+
+def gather_half(value, groups, bits):
+    done = []
+    for bit in bits:
+        axis = sum(b > bit for b in done)
+        value = jnp.stack([value, swap(value, groups, bit)], axis=axis)
+        done.append(bit)
+    return value
+
+
+def scatter(keep, send, groups):
+    total = keep + swap(send, groups, 0)
+    bits = list(range(1, groups.bit_length() - 1))
+    total = total.reshape((2,) * len(bits) + keep.shape[1:])
+    cut = keep.shape[2] // 2
+    axis = len(bits) + 1
+    first = scatter_half(lax.slice_in_dim(total, 0, cut, axis=axis), groups, bits)
+    second = scatter_half(lax.slice_in_dim(total, cut, None, axis=axis), groups, bits[::-1])
+    return jnp.concatenate([first, second], axis=1)
+
+
+def gather(value, groups):
+    bits = list(range(1, groups.bit_length() - 1))
+    cut = value.shape[1] // 2
+    first = gather_half(value[:, :cut], groups, bits)
+    second = gather_half(value[:, cut:], groups, bits[::-1])
+    own = jnp.concatenate([first, second], axis=len(bits) + 1)
+    own = own.reshape((groups // 2,) + value.shape)
+    return own, swap(own, groups, 0)
+
+
 def body(reflection, focusing_input, direct_wave, mute_source, mute_receiver):
     freq_devices = lax.axis_size("freq")
     groups = lax.axis_size("rcv")
     local, _, sources, receivers = reflection.shape
     freqs = local * freq_devices
     share, own = mute_source.shape
-    points = share * groups
     width = min(LANES, own)
     chunks = own // width
     to_time, to_freq = tables(freqs)
     refl = reflection.reshape(local, 2, freq_devices, own, receivers)
     focus = focusing_input.reshape(local, 2, groups, share, receivers)
-    focus = focus.transpose(0, 2, 1, 3, 4).reshape(local, 2 * points, receivers)
+    focus = focus.transpose(0, 2, 1, 3, 4).reshape(local, groups, 2 * share, receivers)
+    me = lax.axis_index("rcv").astype(jnp.int32).reshape(1)
 
     specs = []
     for chunk in range(chunks):
-        term = forward(refl, focus, chunk, width, groups, share)
-        summed = lax.psum_scatter(term, "rcv", scatter_dimension=0, tiled=False)
+        keep, send = forward(me, refl, focus, chunk, width, groups, share)
+        summed = scatter(keep, send, groups)
         spec = lax.all_to_all(summed, "freq", split_axis=0, concat_axis=0, tiled=True)
         specs.append(spec.reshape(freqs, 2 * share, width))
     traces = None
@@ -269,10 +328,10 @@
         )
         back = back.reshape(freq_devices, local, 2 * share, width)
         back = lax.all_to_all(back, "freq", split_axis=0, concat_axis=0, tiled=True)
-        gathered.append(lax.all_gather(back, "rcv", axis=0, tiled=False))
+        gathered.append(gather(back, groups))
     panel = None
     for chunk in range(chunks):
-        panel = adjoint(refl, gathered[chunk], panel, chunk, width, groups, share)
+        panel = adjoint(me, refl, *gathered[chunk], panel, chunk, width, groups, share)
     panel = lax.all_to_all(panel, "freq", split_axis=0, concat_axis=0, tiled=True)
     panel = panel.reshape(freqs, groups // freq_devices * 2 * share, receivers)
     return traces, final(to_time, mute_receiver, panel, direct_wave, share)

time: 311 us -> 273 us (0.88)
  blocking collectives: 125 us -> 53.6 us
  starting transfers between devices: 0.16 us -> 39.5 us
  between operations: 13.9 us -> 0.97 us
  waiting for transfers between devices: 64.2 us -> 75.2 us
  local copies, waits for them, and re-layouts: 13.9 us -> 6.03 us
  other arithmetic: 0 us -> 4.3 us
    all_to_all x4 -> x0, blocking collectives: 71.7 us -> none  [the longest x2 38.2 us: body(): lax.all_to_all(summed, 'freq', split_axis=0, concat_axis=0, tiled=True)]
    ppermute x0 -> x20, waiting for transfers between devices: none -> 50.6 us  [swap(): lax.ppermute(value, 'rcv', [(i, i ^ 1 << bit) for i in range(groups)])]
    reduce_scatter x2 -> x0, waiting for transfers between devices: 46.8 us -> none  [body(): summed = lax.psum_scatter(term, 'rcv', scatter_dimension=0, tiled=False)]
    all_to_all x0 -> x4, waiting for transfers between devices: none -> 24.6 us  [the longest x2 14.3 us: body(): lax.all_to_all(summed, 'freq', split_axis=0, concat_axis=0, tiled=True)]
    ppermute x0 -> x20, starting transfers between devices: none -> 24.2 us  [swap(): lax.ppermute(value, 'rcv', [(i, i ^ 1 << bit) for i in range(groups)])]
    all_gather x2 -> x0, waiting for transfers between devices: 17.3 us -> none  [body(): gathered.append(lax.all_gather(back, 'rcv', axis=0, tiled=False))]
    all_to_all x0 -> x4, starting transfers between devices: none -> 15.3 us  [the longest x2 8.35 us: body(): lax.all_to_all(summed, 'freq', split_axis=0, concat_axis=0, tiled=True)]
    unnamed x18 -> x10, local copies, waits for them, and re-layouts: 8.32 us -> 0.02 us
  transfers between devices with their start and end apart: 4 -> 24, of which waited for: 4 -> 15; matrix products, arithmetic and copies ran while one was open for 0% -> 2% of each run, Pallas kernels for 15% -> 17%
where the time goes in v2:
time: 273 us; the launch traced here: 272 us
  Pallas kernels  92.1 us (34%)
  waiting for transfers between devices  75.2 us (28%)
  blocking collectives  53.6 us (20%)
  starting transfers between devices  39.5 us (14%)
  local copies, waits for them, and re-layouts  6.03 us (2%)
  other arithmetic  4.3 us (2%)
    all_to_all x1, blocking collectives, body(): lax.all_to_all(panel, 'freq', split_axis=0, concat_axis=0, tiled=True)  53.6 us
    ppermute x20, waiting for transfers between devices, swap(): lax.ppermute(value, 'rcv', [(i, i ^ 1 << bit) for i in range(groups)])  50.6 us
    pallas_call x2, Pallas kernels, forward(): pl.pallas_call(functools.partial(forward_kernel, share), grid=(freqs // s...  42.4 us
    pallas_call x2, Pallas kernels, adjoint(): pl.pallas_call(functools.partial(adjoint_kernel, share), grid=(freqs // s...  38 us
    ppermute x20, starting transfers between devices, swap(): lax.ppermute(value, 'rcv', [(i, i ^ 1 << bit) for i in range(groups)])  24.2 us
    all_to_all x2, waiting for transfers between devices, body(): lax.all_to_all(summed, 'freq', split_axis=0, concat_axis=0, tiled=True)  14.3 us
    all_to_all x2, waiting for transfers between devices, body(): back = lax.all_to_all(back, 'freq', split_axis=0, concat_axis=0, tiled=True)  10.3 us
    all_to_all x2, starting transfers between devices, body(): lax.all_to_all(summed, 'freq', split_axis=0, concat_axis=0, tiled=True)  8.35 us
  transfers between devices with their start and end apart: 24, of which 15 were waited for; matrix products, arithmetic and copies ran while one was open for 2% of the time, Pallas kernels for 17%

profile of v2, /device:TPU:0, one launch (start us, length us, event | category | flops | bytes accessed | tf_op | source)
XLA Modules:
  0.0 271.7 jit_solution(9934935250565757510)
XLA Ops:
  0.6 1.9 reshape.45
  2.5 1.8 copy.18
  4.3 2.0 reshape.46.focus_ref
  6.2 21.2 %forward.3 = (f32[4,4,32,8,128]{4,3,2,1,0:T(8,128)S(1)}, f32[4,4,32,8,128]{4,3,2,1,0:T(8,128)S(1)}) custom-call(s32[1]{0:T(128)} %bitcast.me_ref, f32[32,2,4,256,256]{4,3,2,1,0:T(8,128)} %bitcast.1.refl_ref, f32[32,8,8,256]{3,2,1,0:T(8,128)S(1)} %reshape.46.focus_ref), custom_call_target="tpu_custom_call" | custom-call | flops 6442450944 | bytes 37748736 | tf_op jit(solution)/shard_map/forward/pallas_call | solution.py:74
  28.0 21.2 %forward.2 = (f32[4,4,32,8,128]{4,3,2,1,0:T(8,128)S(1)}, f32[4,4,32,8,128]{4,3,2,1,0:T(8,128)S(1)}) custom-call(s32[1]{0:T(128)} %bitcast.me_ref, f32[32,2,4,256,256]{4,3,2,1,0:T(8,128)} %bitcast.1.refl_ref, f32[32,8,8,256]{3,2,1,0:T(8,128)S(1)} %reshape.46.focus_ref), custom_call_target="tpu_custom_call" | custom-call | flops 6442450944 | bytes 37748736 | tf_op jit(solution)/shard_map/forward/pallas_call | solution.py:74
  49.6 3.0 %collective-permute-start.6 = (f32[2,4,16,8,128]{4,3,2,1,0:T(8,128)S(1)}, f32[2,4,16,8,128]{4,3,2,1,0:T(8,128)S(1)}, u32[]{:S(2)}, u32[]{:S(2)}) collective-permute-start(f32[2,4,16,8,128]{4,3,2,1,0:T(8,128)S(1)} %slice_bitcast_fusion.2), channel_id=1, source_target_pairs={{0,2},{1,3},{2,0},{3,1},{4,6},{5,7},{6,4},{7,5},{8,10},{9,11},{10,... | collective-permute-start | bytes 1572872 | tf_op jit(solution)/shard_map/ppermute | solution.py:260
  52.6 1.5 collective-permute-start.8
  54.5 1.9 collective-permute-start.1
  56.5 1.6 collective-permute-start.3
  58.0 7.3 %collective-permute-done.6 = f32[2,4,16,8,128]{4,3,2,1,0:T(8,128)S(1)} collective-permute-done((f32[2,4,16,8,128]{4,3,2,1,0:T(8,128)S(1)}, f32[2,4,16,8,128]{4,3,2,1,0:T(8,128)S(1)}, u32[]{:S(2)}, u32[]{:S(2)}) %collective-permute-start.6) | collective-permute-done | bytes 524320 | tf_op jit(solution)/shard_map/ppermute | solution.py:260
  65.4 2.1 collective-permute-done.8
  67.6 1.6 collective-permute-start.7
  69.8 6.8 %collective-permute-done.1 = f32[2,4,16,8,128]{4,3,2,1,0:T(8,128)S(1)} collective-permute-done((f32[2,4,16,8,128]{4,3,2,1,0:T(8,128)S(1)}, f32[2,4,16,8,128]{4,3,2,1,0:T(8,128)S(1)}, u32[]{:S(2)}, u32[]{:S(2)}) %collective-permute-start.1) | collective-permute-done | bytes 524320 | tf_op jit(solution)/shard_map/ppermute | solution.py:260
  76.6 2.1 collective-permute-done.3
  78.8 1.6 collective-permute-start.2
  80.4 3.9 %collective-permute-done.7 = f32[4,16,8,128]{3,2,1,0:T(8,128)S(1)} collective-permute-done((f32[4,16,8,128]{3,2,1,0:T(8,128)S(1)}, f32[4,16,8,128]{3,2,1,0:T(8,128)S(1)}, u32[]{:S(2)}, u32[]{:S(2)}) %collective-permute-start.7) | collective-permute-done | bytes 262176 | tf_op jit(solution)/shard_map/ppermute | solution.py:260
  84.4 0.8 pad_maximum_fusion.1
  85.2 4.9 %all-to-all-start.1 = ((f32[4,32,8,128]{3,2,1,0:T(8,128)}), f32[4,32,8,128]{3,2,1,0:T(8,128)S(1)}, u32[]{:S(2)}, u32[]{:S(2)}) async-start(f32[4,32,8,128]{3,2,1,0:T(8,128)} %pad_maximum_fusion.1), calls=%async_computation.1 | async-start | bytes 1048576 | tf_op jit(solution)/shard_map/all_to_all | solution.py:321
  90.1 0.6 collective-permute-start.4
  90.8 5.8 %collective-permute-done.4 = f32[4,16,8,128]{3,2,1,0:T(8,128)S(1)} collective-permute-done((f32[4,16,8,128]{3,2,1,0:T(8,128)S(1)}, f32[4,16,8,128]{3,2,1,0:T(8,128)S(1)}, u32[]{:S(2)}, u32[]{:S(2)}) %collective-permute-start.4) | collective-permute-done | bytes 262176 | tf_op jit(solution)/shard_map/ppermute | solution.py:260
  96.6 0.8 pad_maximum_fusion
  97.4 4.9 %all-to-all-done.1 = f32[4,32,8,128]{3,2,1,0:T(8,128)S(1)} async-done(((f32[4,32,8,128]{3,2,1,0:T(8,128)}), f32[4,32,8,128]{3,2,1,0:T(8,128)S(1)}, u32[]{:S(2)}, u32[]{:S(2)}) %all-to-all-start.1) | async-done | bytes 524320 | tf_op jit(solution)/shard_map/all_to_all | solution.py:321
  102.4 3.5 %all-to-all-start = ((f32[4,32,8,128]{3,2,1,0:T(8,128)}), f32[4,32,8,128]{3,2,1,0:T(8,128)S(1)}, u32[]{:S(2)}, u32[]{:S(2)}) async-start(f32[4,32,8,128]{3,2,1,0:T(8,128)} %pad_maximum_fusion), calls=%async_computation | async-start | bytes 1048576 | tf_op jit(solution)/shard_map/all_to_all | solution.py:321
  105.9 2.9 %window_source.2 = (f32[256,4,256]{2,1,0:T(4,128)}, f32[128,8,128]{2,1,0:T(8,128)}) custom-call(bf16[2,256,256]{2,1,0:T(8,128)(2,1)S(1)} %copy-done.1, bf16[2,256,256]{2,1,0:T(8,128)(2,1)S(1)} %copy-done.2, s32[4,256]{1,0:T(4,128)S(1)} %copy-done.4, f32[128,8,128]{2,1,0:T(8,128)S(1)} %bitcast.102), custom_call_target="tpu_custom_call" | custom-call | flops 402653184 | bytes 1572864 | tf_op jit(solution)/shard_map/window_source/pallas_call | solution.py:183
  108.7 9.3 %all-to-all-done = f32[4,32,8,128]{3,2,1,0:T(8,128)S(1)} async-done(((f32[4,32,8,128]{3,2,1,0:T(8,128)}), f32[4,32,8,128]{3,2,1,0:T(8,128)S(1)}, u32[]{:S(2)}, u32[]{:S(2)}) %all-to-all-start) | async-done | bytes 524320 | tf_op jit(solution)/shard_map/all_to_all | solution.py:321
  118.1 3.5 %all-to-all-start.3 = ((f32[4,32,8,128]{3,2,1,0:T(8,128)}), f32[4,32,8,128]{3,2,1,0:T(8,128)S(1)}, u32[]{:S(2)}, u32[]{:S(2)}) async-start(f32[4,32,8,128]{3,2,1,0:T(8,128)} %bitcast.34), calls=%async_computation.3 | async-start | bytes 1048576 | tf_op jit(solution)/shard_map/all_to_all | solution.py:330
  121.6 2.9 %window_source.3 = (f32[256,4,256]{2,1,0:T(4,128)}, f32[128,8,128]{2,1,0:T(8,128)}) custom-call(bf16[2,256,256]{2,1,0:T(8,128)(2,1)S(1)} %copy-done.1, bf16[2,256,256]{2,1,0:T(8,128)(2,1)S(1)} %copy-done.2, s32[4,256]{1,0:T(4,128)S(1)} %copy-done.4, f32[128,8,128]{2,1,0:T(8,128)S(1)} %bitcast.101, ...), custom_call_target="tpu_custom_call", output_to_operand_aliasing={{0}: (4, {})} | custom-call | flops 402653184 | bytes 1572864 | tf_op jit(solution)/shard_map/window_source/pallas_call | solution.py:183
  124.4 9.4 %all-to-all-done.3 = f32[4,32,8,128]{3,2,1,0:T(8,128)S(1)} async-done(((f32[4,32,8,128]{3,2,1,0:T(8,128)}), f32[4,32,8,128]{3,2,1,0:T(8,128)S(1)}, u32[]{:S(2)}, u32[]{:S(2)}) %all-to-all-start.3) | async-done | bytes 524320 | tf_op jit(solution)/shard_map/all_to_all | solution.py:330
  133.8 3.5 %all-to-all-start.2 = ((f32[4,32,8,128]{3,2,1,0:T(8,128)}), f32[4,32,8,128]{3,2,1,0:T(8,128)S(1)}, u32[]{:S(2)}, u32[]{:S(2)}) async-start(f32[4,32,8,128]{3,2,1,0:T(8,128)} %bitcast.23), calls=%async_computation.2 | async-start | bytes 1048576 | tf_op jit(solution)/shard_map/all_to_all | solution.py:330
  137.4 0.6 collective-permute-start.15
  138.0 1.5 collective-permute-start.17
  139.5 4.3 %collective-permute-done.15 = f32[4,16,8,128]{3,2,1,0:T(8,128)S(1)} collective-permute-done((f32[4,16,8,128]{3,2,1,0:T(8,128)S(1)}, f32[4,16,8,128]{3,2,1,0:T(8,128)S(1)}, u32[]{:S(2)}, u32[]{:S(2)}) %collective-permute-start.15) | collective-permute-done | bytes 262176 | tf_op jit(solution)/shard_map/ppermute | solution.py:260
  143.9 2.2 collective-permute-start.16
  146.2 2.3 collective-permute-start.18
  148.6 1.0 all-to-all-done.2
  149.7 0.6 collective-permute-start.10
  150.3 1.5 collective-permute-start.12
  151.8 9.2 %collective-permute-done.10 = f32[4,16,8,128]{3,2,1,0:T(8,128)S(1)} collective-permute-done((f32[4,16,8,128]{3,2,1,0:T(8,128)S(1)}, f32[4,16,8,128]{3,2,1,0:T(8,128)S(1)}, u32[]{:S(2)}, u32[]{:S(2)}) %collective-permute-start.10) | collective-permute-done | bytes 262176 | tf_op jit(solution)/shard_map/ppermute | solution.py:260
  161.1 1.2 collective-permute-start.11
  162.4 2.0 collective-permute-done.12
  164.5 0.9 collective-permute-start.13
  165.4 1.2 maximum_maximum_fusion.1
  166.7 5.8 %collective-permute-done.11 = f32[2,4,16,8,128]{4,3,2,1,0:T(8,128)S(1)} collective-permute-done((f32[2,4,16,8,128]{4,3,2,1,0:T(8,128)S(1)}, f32[2,4,16,8,128]{4,3,2,1,0:T(8,128)S(1)}, u32[]{:S(2)}, u32[]{:S(2)}) %collective-permute-start.11) | collective-permute-done | bytes 524320 | tf_op jit(solution)/shard_map/ppermute | solution.py:260
  172.5 1.3 collective-permute-done.13
  174.0 18.9 %adjoint.2.rest_0_ = f32[4,32,2,8,256]{4,3,2,1,0:T(8,128)S(1)} custom-call(s32[1]{0:T(128)} %bitcast.me_ref, f32[32,2,4,256,256]{4,3,2,1,0:T(8,128)} %bitcast.1.refl_ref, f32[4,4,32,8,128]{4,3,2,1,0:T(8,128)S(1)} %bitcast.97, f32[4,4,32,8,128]{4,3,2,1,0:T(8,128)S(1)} %collective-permute-done.19.other_ref), custom_call_target="tpu_custom_call" | custom-call | flops 6442450944 | bytes 37748736 | tf_op jit(solution)/shard_map/adjoint/pallas_call | solution.py:135
  192.9 19.1 %adjoint.3 = f32[4,32,2,8,256]{4,3,2,1,0:T(8,128)S(1)} custom-call(s32[1]{0:T(128)} %bitcast.me_ref, f32[32,2,4,256,256]{4,3,2,1,0:T(8,128)} %bitcast.1.refl_ref, f32[4,4,32,8,128]{4,3,2,1,0:T(8,128)S(1)} %bitcast.99, f32[4,4,32,8,128]{4,3,2,1,0:T(8,128)S(1)} %collective-permute-done.14.other_ref, f32[4,32,2,8,256]{4,3,2,1,0:T(8,128)S(1)} %adjoint.2.rest_0_), custom_call_target="tpu_custom_call" | custom-call | flops 6442450944 | bytes 37748736 | tf_op jit(solution)/shard_map/adjoint/pallas_call | solution.py:135
  212.1 53.6 %all_to_all.25 = f32[4,32,2,8,256]{4,3,2,1,0:T(8,128)S(1)} all-to-all(f32[4,32,2,8,256]{4,3,2,1,0:T(8,128)S(1)} %adjoint.3), channel_id=1, replica_groups=mesh['freq'=4,'rcv'=8] {'freq'}, dimensions={0} | all-to-all | bytes 4194304 | tf_op jit(solution)/shard_map/all_to_all | solution.py:335
  265.7 6.0 %final.1 = f32[256,8,256]{2,1,0:T(8,128)} custom-call(bf16[2,256,256]{2,1,0:T(8,128)(2,1)S(1)} %copy-done.1, s32[8,256]{1,0:T(8,128)S(1)} %copy-done.3, f32[128,16,256]{2,1,0:T(8,128)S(1)} %bitcast.100, f32[256,8,256]{2,1,0:T(8,128)S(1)} %copy-done), custom_call_target="tpu_custom_call" | custom-call | flops 805306368 | bytes 6291456 | tf_op jit(solution)/shard_map/final/pallas_call | solution.py:227
  (47 shorter events, 3.3 us)
Async XLA Ops:
  27.4 21.8 %collective-permute-start.5 = (f32[4,4,32,8,128]{4,3,2,1,0:T(8,128)S(1)}, f32[4,4,32,8,128]{4,3,2,1,0:T(8,128)S(1)}, u32[]{:S(2)}, u32[]{:S(2)}) collective-permute-start(f32[4,4,32,8,128]{4,3,2,1,0:T(8,128)S(1)} %get-tuple-element.13), channel_id=1, source_target_pairs={{0,1},{1,0},{2,3},{3,2},{4,5},{5,4},{6,7},{7,6},{8,9},{9,8},{10,11... | collective-permute-start | bytes 6291464 | tf_op jit(solution)/shard_map/ppermute | solution.py:260
  49.2 5.0 %collective-permute-start = (f32[4,4,32,8,128]{4,3,2,1,0:T(8,128)S(1)}, f32[4,4,32,8,128]{4,3,2,1,0:T(8,128)S(1)}, u32[]{:S(2)}, u32[]{:S(2)}) collective-permute-start(f32[4,4,32,8,128]{4,3,2,1,0:T(8,128)S(1)} %get-tuple-element.11), channel_id=1, source_target_pairs={{0,1},{1,0},{2,3},{3,2},{4,5},{5,4},{6,7},{7,6},{8,9},{9,8},{10,11... | collective-permute-start | bytes 6291464 | tf_op jit(solution)/shard_map/ppermute | solution.py:260
  49.6 15.7 %collective-permute-start.6 = (f32[2,4,16,8,128]{4,3,2,1,0:T(8,128)S(1)}, f32[2,4,16,8,128]{4,3,2,1,0:T(8,128)S(1)}, u32[]{:S(2)}, u32[]{:S(2)}) collective-permute-start(f32[2,4,16,8,128]{4,3,2,1,0:T(8,128)S(1)} %slice_bitcast_fusion.2), channel_id=1, source_target_pairs={{0,2},{1,3},{2,0},{3,1},{4,6},{5,7},{6,4},{7,5},{8,10},{9,11},{10,... | collective-permute-start | bytes 1572872 | tf_op jit(solution)/shard_map/ppermute | solution.py:260
  52.6 14.8 %collective-permute-start.8 = (f32[2,4,16,8,128]{4,3,2,1,0:T(8,128)S(1)}, f32[2,4,16,8,128]{4,3,2,1,0:T(8,128)S(1)}, u32[]{:S(2)}, u32[]{:S(2)}) collective-permute-start(f32[2,4,16,8,128]{4,3,2,1,0:T(8,128)S(1)} %slice_bitcast_fusion), channel_id=1, source_target_pairs={{0,4},{1,5},{2,6},{3,7},{4,0},{5,1},{6,2},{7,3},{8,12},{9,13},{10,... | collective-permute-start | bytes 1572872 | tf_op jit(solution)/shard_map/ppermute | solution.py:260
  54.5 22.1 %collective-permute-start.1 = (f32[2,4,16,8,128]{4,3,2,1,0:T(8,128)S(1)}, f32[2,4,16,8,128]{4,3,2,1,0:T(8,128)S(1)}, u32[]{:S(2)}, u32[]{:S(2)}) collective-permute-start(f32[2,4,16,8,128]{4,3,2,1,0:T(8,128)S(1)} %slice_bitcast_fusion.6), channel_id=1, source_target_pairs={{0,2},{1,3},{2,0},{3,1},{4,6},{5,7},{6,4},{7,5},{8,10},{9,11},{10,... | collective-permute-start | bytes 1572872 | tf_op jit(solution)/shard_map/ppermute | solution.py:260
  56.5 22.2 %collective-permute-start.3 = (f32[2,4,16,8,128]{4,3,2,1,0:T(8,128)S(1)}, f32[2,4,16,8,128]{4,3,2,1,0:T(8,128)S(1)}, u32[]{:S(2)}, u32[]{:S(2)}) collective-permute-start(f32[2,4,16,8,128]{4,3,2,1,0:T(8,128)S(1)} %slice_bitcast_fusion.4), channel_id=1, source_target_pairs={{0,4},{1,5},{2,6},{3,7},{4,0},{5,1},{6,2},{7,3},{8,12},{9,13},{10,... | collective-permute-start | bytes 1572872 | tf_op jit(solution)/shard_map/ppermute | solution.py:260
  67.6 16.7 %collective-permute-start.7 = (f32[4,16,8,128]{3,2,1,0:T(8,128)S(1)}, f32[4,16,8,128]{3,2,1,0:T(8,128)S(1)}, u32[]{:S(2)}, u32[]{:S(2)}) collective-permute-start(f32[4,16,8,128]{3,2,1,0:T(8,128)S(1)} %slice_bitcast_fusion.10), channel_id=1, source_target_pairs={{0,4},{1,5},{2,6},{3,7},{4,0},{5,1},{6,2},{7,3},{8,12},{9,13},{10,... | collective-permute-start | bytes 786440 | tf_op jit(solution)/shard_map/ppermute | solution.py:260
  69.2 15.1 %collective-permute-start.9 = (f32[4,16,8,128]{3,2,1,0:T(8,128)S(1)}, f32[4,16,8,128]{3,2,1,0:T(8,128)S(1)}, u32[]{:S(2)}, u32[]{:S(2)}) collective-permute-start(f32[4,16,8,128]{3,2,1,0:T(8,128)S(1)} %slice_bitcast_fusion.8), channel_id=1, source_target_pairs={{0,2},{1,3},{2,0},{3,1},{4,6},{5,7},{6,4},{7,5},{8,10},{9,11},{10,... | collective-permute-start | bytes 786440 | tf_op jit(solution)/shard_map/ppermute | solution.py:260
  78.8 11.9 %collective-permute-start.2 = (f32[4,16,8,128]{3,2,1,0:T(8,128)S(1)}, f32[4,16,8,128]{3,2,1,0:T(8,128)S(1)}, u32[]{:S(2)}, u32[]{:S(2)}) collective-permute-start(f32[4,16,8,128]{3,2,1,0:T(8,128)S(1)} %slice_bitcast_fusion.14), channel_id=1, source_target_pairs={{0,4},{1,5},{2,6},{3,7},{4,0},{5,1},{6,2},{7,3},{8,12},{9,13},{10,... | collective-permute-start | bytes 786440 | tf_op jit(solution)/shard_map/ppermute | solution.py:260
  85.2 17.1 %all-to-all-start.1 = ((f32[4,32,8,128]{3,2,1,0:T(8,128)}), f32[4,32,8,128]{3,2,1,0:T(8,128)S(1)}, u32[]{:S(2)}, u32[]{:S(2)}) async-start(f32[4,32,8,128]{3,2,1,0:T(8,128)} %pad_maximum_fusion.1), calls=%async_computation.1 | async-start | bytes 1048576 | tf_op jit(solution)/shard_map/all_to_all | solution.py:321
  90.1 15.7 %copy-start.1 = (bf16[2,256,256]{2,1,0:T(8,128)(2,1)S(1)}, bf16[2,256,256]{2,1,0:T(8,128)(2,1)}, u32[]{:S(2)}) copy-start(bf16[2,256,256]{2,1,0:T(8,128)(2,1)} %constant.8.clone.to_time) | copy-start | bytes 786436
  90.1 15.8 %copy-start.2 = (bf16[2,256,256]{2,1,0:T(8,128)(2,1)S(1)}, bf16[2,256,256]{2,1,0:T(8,128)(2,1)}, u32[]{:S(2)}) copy-start(bf16[2,256,256]{2,1,0:T(8,128)(2,1)} %constant.9.clone.to_freq) | copy-start | bytes 786436
  90.1 15.8 %copy-start.4 = (s32[4,256]{1,0:T(4,128)S(1)}, s32[4,256]{1,0:T(4,128)}, u32[]{:S(2)}) copy-start(s32[4,256]{1,0:T(4,128)} %mute_ref.4) | copy-start | bytes 12292
  90.1 6.4 %collective-permute-start.4 = (f32[4,16,8,128]{3,2,1,0:T(8,128)S(1)}, f32[4,16,8,128]{3,2,1,0:T(8,128)S(1)}, u32[]{:S(2)}, u32[]{:S(2)}) collective-permute-start(f32[4,16,8,128]{3,2,1,0:T(8,128)S(1)} %slice_bitcast_fusion.12), channel_id=1, source_target_pairs={{0,2},{1,3},{2,0},{3,1},{4,6},{5,7},{6,4},{7,5},{8,10},{9,11},{10,... | collective-permute-start | bytes 786440 | tf_op jit(solution)/shard_map/ppermute | solution.py:260
  102.4 15.7 %all-to-all-start = ((f32[4,32,8,128]{3,2,1,0:T(8,128)}), f32[4,32,8,128]{3,2,1,0:T(8,128)S(1)}, u32[]{:S(2)}, u32[]{:S(2)}) async-start(f32[4,32,8,128]{3,2,1,0:T(8,128)} %pad_maximum_fusion), calls=%async_computation | async-start | bytes 1048576 | tf_op jit(solution)/shard_map/all_to_all | solution.py:321
  118.1 15.7 %all-to-all-start.3 = ((f32[4,32,8,128]{3,2,1,0:T(8,128)}), f32[4,32,8,128]{3,2,1,0:T(8,128)S(1)}, u32[]{:S(2)}, u32[]{:S(2)}) async-start(f32[4,32,8,128]{3,2,1,0:T(8,128)} %bitcast.34), calls=%async_computation.3 | async-start | bytes 1048576 | tf_op jit(solution)/shard_map/all_to_all | solution.py:330
  133.8 15.7 %all-to-all-start.2 = ((f32[4,32,8,128]{3,2,1,0:T(8,128)}), f32[4,32,8,128]{3,2,1,0:T(8,128)S(1)}, u32[]{:S(2)}, u32[]{:S(2)}) async-start(f32[4,32,8,128]{3,2,1,0:T(8,128)} %bitcast.23), calls=%async_computation.2 | async-start | bytes 1048576 | tf_op jit(solution)/shard_map/all_to_all | solution.py:330
  137.4 6.4 %collective-permute-start.15 = (f32[4,16,8,128]{3,2,1,0:T(8,128)S(1)}, f32[4,16,8,128]{3,2,1,0:T(8,128)S(1)}, u32[]{:S(2)}, u32[]{:S(2)}) collective-permute-start(f32[4,16,8,128]{3,2,1,0:T(8,128)S(1)} %get-tuple-element.27), channel_id=1, source_target_pairs={{0,2},{1,3},{2,0},{3,1},{4,6},{5,7},{6,4},{7,5},{8,10},{9,11},{10,... | collective-permute-start | bytes 786440 | tf_op jit(solution)/shard_map/ppermute | solution.py:260
  138.0 8.1 %collective-permute-start.17 = (f32[4,16,8,128]{3,2,1,0:T(8,128)S(1)}, f32[4,16,8,128]{3,2,1,0:T(8,128)S(1)}, u32[]{:S(2)}, u32[]{:S(2)}) collective-permute-start(f32[4,16,8,128]{3,2,1,0:T(8,128)S(1)} %get-tuple-element.26), channel_id=1, source_target_pairs={{0,4},{1,5},{2,6},{3,7},{4,0},{5,1},{6,2},{7,3},{8,12},{9,13},{10,... | collective-permute-start | bytes 786440 | tf_op jit(solution)/shard_map/ppermute | solution.py:260
  143.9 21.5 %collective-permute-start.16 = (f32[2,4,16,8,128]{4,3,2,1,0:T(8,128)S(1)}, f32[2,4,16,8,128]{4,3,2,1,0:T(8,128)S(1)}, u32[]{:S(2)}, u32[]{:S(2)}) collective-permute-start(f32[2,4,16,8,128]{4,3,2,1,0:T(8,128)S(1)} %get-tuple-element.23), channel_id=1, source_target_pairs={{0,4},{1,5},{2,6},{3,7},{4,0},{5,1},{6,2},{7,3},{8,12},{9,13},{10,... | collective-permute-start | bytes 1572872 | tf_op jit(solution)/shard_map/ppermute | solution.py:260
  146.2 19.2 %collective-permute-start.18 = (f32[2,4,16,8,128]{4,3,2,1,0:T(8,128)S(1)}, f32[2,4,16,8,128]{4,3,2,1,0:T(8,128)}, u32[]{:S(2)}, u32[]{:S(2)}) collective-permute-start(f32[2,4,16,8,128]{4,3,2,1,0:T(8,128)S(1)} %get-tuple-element.29), channel_id=1, source_target_pairs={{0,2},{1,3},{2,0},{3,1},{4,6},{5,7},{6,4},{7,5},{8,10},{9,11},{10,... | collective-permute-start | bytes 1572872 | tf_op jit(solution)/shard_map/ppermute | solution.py:260
  149.7 11.4 %collective-permute-start.10 = (f32[4,16,8,128]{3,2,1,0:T(8,128)S(1)}, f32[4,16,8,128]{3,2,1,0:T(8,128)S(1)}, u32[]{:S(2)}, u32[]{:S(2)}) collective-permute-start(f32[4,16,8,128]{3,2,1,0:T(8,128)S(1)} %get-tuple-element.35), channel_id=1, source_target_pairs={{0,2},{1,3},{2,0},{3,1},{4,6},{5,7},{6,4},{7,5},{8,10},{9,11},{10,... | collective-permute-start | bytes 786440 | tf_op jit(solution)/shard_map/ppermute | solution.py:260
  150.3 14.1 %collective-permute-start.12 = (f32[4,16,8,128]{3,2,1,0:T(8,128)S(1)}, f32[4,16,8,128]{3,2,1,0:T(8,128)S(1)}, u32[]{:S(2)}, u32[]{:S(2)}) collective-permute-start(f32[4,16,8,128]{3,2,1,0:T(8,128)S(1)} %get-tuple-element.34), channel_id=1, source_target_pairs={{0,4},{1,5},{2,6},{3,7},{4,0},{5,1},{6,2},{7,3},{8,12},{9,13},{10,... | collective-permute-start | bytes 786440 | tf_op jit(solution)/shard_map/ppermute | solution.py:260
  161.1 11.3 %collective-permute-start.11 = (f32[2,4,16,8,128]{4,3,2,1,0:T(8,128)S(1)}, f32[2,4,16,8,128]{4,3,2,1,0:T(8,128)S(1)}, u32[]{:S(2)}, u32[]{:S(2)}) collective-permute-start(f32[2,4,16,8,128]{4,3,2,1,0:T(8,128)S(1)} %get-tuple-element.31), channel_id=1, source_target_pairs={{0,4},{1,5},{2,6},{3,7},{4,0},{5,1},{6,2},{7,3},{8,12},{9,13},{10,... | collective-permute-start | bytes 1572872 | tf_op jit(solution)/shard_map/ppermute | solution.py:260
  164.5 9.2 %collective-permute-start.13 = (f32[2,4,16,8,128]{4,3,2,1,0:T(8,128)S(1)}, f32[2,4,16,8,128]{4,3,2,1,0:T(8,128)S(1)}, u32[]{:S(2)}, u32[]{:S(2)}) collective-permute-start(f32[2,4,16,8,128]{4,3,2,1,0:T(8,128)S(1)} %get-tuple-element.37), channel_id=1, source_target_pairs={{0,2},{1,3},{2,0},{3,1},{4,6},{5,7},{6,4},{7,5},{8,10},{9,11},{10,... | collective-permute-start | bytes 1572872 | tf_op jit(solution)/shard_map/ppermute | solution.py:260
  166.6 7.4 %collective-permute-start.19 = (f32[4,4,32,8,128]{4,3,2,1,0:T(8,128)S(1)}, f32[4,4,32,8,128]{4,3,2,1,0:T(8,128)S(1)}, u32[]{:S(2)}, u32[]{:S(2)}) collective-permute-start(f32[4,4,32,8,128]{4,3,2,1,0:T(8,128)S(1)} %bitcast.96), channel_id=1, source_target_pairs={{0,1},{1,0},{2,3},{3,2},{4,5},{5,4},{6,7},{7,6},{8,9},{9,8},{10,11... | collective-permute-start | bytes 6291464 | tf_op jit(solution)/shard_map/ppermute | solution.py:260
  173.9 19.0 %collective-permute-start.14 = (f32[4,4,32,8,128]{4,3,2,1,0:T(8,128)S(1)}, f32[4,4,32,8,128]{4,3,2,1,0:T(8,128)S(1)}, u32[]{:S(2)}, u32[]{:S(2)}) collective-permute-start(f32[4,4,32,8,128]{4,3,2,1,0:T(8,128)S(1)} %bitcast.98), channel_id=1, source_target_pairs={{0,1},{1,0},{2,3},{3,2},{4,5},{5,4},{6,7},{7,6},{8,9},{9,8},{10,11... | collective-permute-start | bytes 6291464 | tf_op jit(solution)/shard_map/ppermute | solution.py:260
  212.0 53.7 %copy-start = (f32[256,8,256]{2,1,0:T(8,128)S(1)}, f32[256,8,256]{2,1,0:T(8,128)}, u32[]{:S(2)}) copy-start(f32[256,8,256]{2,1,0:T(8,128)} %direct_ref.1) | copy-start | bytes 6291460
  212.0 53.7 %copy-start.3 = (s32[8,256]{1,0:T(8,128)S(1)}, s32[8,256]{1,0:T(8,128)}, u32[]{:S(2)}) copy-start(s32[8,256]{1,0:T(8,128)} %mute_ref.5) | copy-start | bytes 24580
